TPU v7x, 128 devices: a whole 4x4x4 slice. The times are simulated.
128 devices in a mesh: group: 8 (over z, core), local: 16 (over y, x).
Axes of the slice: x: 4, y: 4, z: 4, core: 2. Of those that a mesh axis runs over, the one named last changes fastest.
Arguments:
- tokens: bfloat16 [512, 7168], P('local'), may hold values from -6 to 6
- cotangent: bfloat16 [512, 7168], P('local'), may hold values from -6 to 6
- gate_logits: float32 [512, 24], P('local'), may hold values from -8 to 8
- route_slot: int32 [512, 8], P('local'), may hold values from 0 to 31, all different within a row; in each aligned block of 32 rows (0 to 31, 32 to 63, ...) at most 16 rows name the same one
- slot_expert: int32 [32], replicated, may hold values from 0 to 23, as said below
- w_gate: bfloat16 [32, 7168, 1024], P('local', None, 'group')
- w_up: bfloat16 [32, 7168, 1024], P('local', None, 'group')
- w_down: bfloat16 [32, 1024, 7168], P('local', 'group'), as said below
Outputs:
- mixed: bfloat16 [512, 7168], P('local', 'group')
- grad_tokens: bfloat16 [512, 7168], P('local', 'group')
- grad_logits: float32 [512, 24], P('local')
- grad_gate: bfloat16 [32, 7168, 1024], P('local', None, 'group')
- grad_up: bfloat16 [32, 7168, 1024], P('local', None, 'group')
- grad_down: bfloat16 [32, 1024, 7168], P('local', 'group')
Inputs may be any that keep to these rules, and one draw needn't show every extreme that they name: `route_slot`: each token names 8 different slots. Of the 32 tokens of one index of local, at most 16 name one slot, a bound that some block reaches of them. `slot_expert`: the even slots hold 16 different experts, the odd slots the remaining ones, each on two odd slots: slot 2i + 1 and slot 2j + 1 hold the same expert where j = i plus or minus half the size of local (the one that stays in range). Every expert is held. `w_down`: two odd slots that hold the same expert have equal weights; entries have standard deviation 1024 ** -0.5.
All inputs are finite; a program needn't handle non-finite values.
Results may differ from a plain program's by a relative error of at most 0.019.
Values may be sent and summed in bfloat16 or wider, within the bound.
No kernel may reach another device: no remote copies, remote signals or barrier semaphores. Data moves between devices by JAX's collectives and lax.ppermute only.
A program may use at most 192 MiB of HBM per device.

v0:
```python
import jax
import jax.numpy as jnp
from jax import lax
from jax.sharding import PartitionSpec as P

ROUTE_SCALE = 2.5
CONTRACT_ONE = (((1,), (1,)), ((), ()))
CONTRACT_ZERO = (((0,), (0,)), ((), ()))


def swapped(block, axis, apart):
    count = lax.axis_size(axis)
    route = []
    for low in range(count):
        high = low | 1 << apart
        if high != low and high < count:
            route += [(low, high), (high, low)]
    return lax.ppermute(block, axis, route)


def gate_weights(logits, expert_ids, experts):
    match = expert_ids[:, :, None] == jnp.arange(experts, dtype=jnp.int32)[None, None, :]
    picked = jnp.sum(jnp.where(match, logits[:, None, :], 0.0), axis=2)
    sig = jax.nn.sigmoid(picked)
    return ROUTE_SCALE * sig / jnp.sum(sig, axis=1, keepdims=True)


def activations(rows_x, rows_g, w_g, w_u, w_d):
    first = jnp.dot(rows_x, w_g, preferred_element_type=jnp.float32)
    second = jnp.dot(rows_x, w_u, preferred_element_type=jnp.float32)
    sig = jax.nn.sigmoid(first)
    silu = first * sig
    hidden = (silu * second).astype(jnp.bfloat16)
    back = lax.dot_general(rows_g, w_d, CONTRACT_ONE, preferred_element_type=jnp.float32)
    d_first = (back * second * sig * (1.0 + first * (1.0 - sig))).astype(jnp.bfloat16)
    d_second = (back * silu).astype(jnp.bfloat16)
    return (hidden, d_first, d_second)


def weight_grads(rows_x, rows_g, hidden, d_first, d_second):
    own_gate = lax.dot_general(rows_x, d_first, CONTRACT_ZERO, preferred_element_type=jnp.float32)
    own_up = lax.dot_general(rows_x, d_second, CONTRACT_ZERO, preferred_element_type=jnp.float32)
    own_down = lax.dot_general(hidden, rows_g, CONTRACT_ZERO, preferred_element_type=jnp.float32)
    return (
        own_gate.astype(jnp.bfloat16),
        own_up.astype(jnp.bfloat16),
        own_down.astype(jnp.bfloat16),
    )


def slot_pass(rows_x, rows_g, w_g, w_u, w_d):
    hidden, d_first, d_second = activations(rows_x, rows_g, w_g, w_u, w_d)
    out_rows = jnp.dot(hidden, w_d, preferred_element_type=jnp.float32).astype(jnp.bfloat16)
    both = lax.dot_general(d_first, w_g, CONTRACT_ONE, preferred_element_type=jnp.float32)
    both = both + lax.dot_general(d_second, w_u, CONTRACT_ONE, preferred_element_type=jnp.float32)
    grad_rows = both.astype(jnp.bfloat16)
    return (out_rows, grad_rows, weight_grads(rows_x, rows_g, hidden, d_first, d_second))


def per_device(tokens, cotangent, gate_logits, route_slot, slot_expert, w_gate, w_up, w_down):
    tok = tokens.shape[0]
    width = tokens.shape[1]
    top = route_slot.shape[1]
    slots = slot_expert.shape[0]
    experts = gate_logits.shape[1]
    lines = lax.axis_size("local")
    cap = top * tok // lines
    match_slot = route_slot[:, :, None] == jnp.arange(slots, dtype=jnp.int32)[None, None, :]
    expert_ids = jnp.sum(jnp.where(match_slot, slot_expert[None, None, :], 0), axis=2)
    weights, pull_back = jax.vjp(lambda lg: gate_weights(lg, expert_ids, experts), gate_logits)
    scaled = (weights[:, :, None] * cotangent.astype(jnp.float32)[:, None, :]).astype(jnp.bfloat16)
    flat = route_slot.reshape(-1)
    onehot = (flat[:, None] == jnp.arange(slots, dtype=jnp.int32)[None, :]).astype(jnp.int32)
    rank = jnp.sum((jnp.cumsum(onehot, axis=0) - onehot) * onehot, axis=1)
    target = flat * cap + rank
    placer = (jnp.arange(slots * cap, dtype=jnp.int32)[:, None] == target[None, :]).astype(
        jnp.bfloat16
    )
    token_placer = jnp.sum(placer.reshape(slots * cap, tok, top), axis=2)
    x_buffer = jnp.dot(token_placer, tokens, preferred_element_type=jnp.float32).astype(
        jnp.bfloat16
    )
    g_buffer = jnp.dot(
        placer, scaled.reshape(tok * top, width), preferred_element_type=jnp.float32
    ).astype(jnp.bfloat16)
    x_buffer = x_buffer.reshape(lines, 2 * cap, width)
    g_buffer = g_buffer.reshape(lines, 2 * cap, width)
    got_x, got_g = (
        lax.all_to_all(x_buffer, "local", split_axis=0, concat_axis=0, tiled=True),
        lax.all_to_all(g_buffer, "local", split_axis=0, concat_axis=0, tiled=True),
    )
    got_x = got_x.reshape(lines, 2, cap, width)
    got_g = got_g.reshape(lines, 2, cap, width)
    rows_cold_x = got_x[:, 0].reshape(lines * cap, width)
    rows_cold_g = got_g[:, 0].reshape(lines * cap, width)
    rows_hot_x = got_x[:, 1].reshape(lines * cap, width)
    rows_hot_g = got_g[:, 1].reshape(lines * cap, width)
    out_cold, dx_cold, grads_cold = slot_pass(
        rows_cold_x, rows_cold_g, w_gate[0], w_up[0], w_down[0]
    )
    out_hot, dx_hot, grads_hot = slot_pass(rows_hot_x, rows_hot_g, w_gate[1], w_up[1], w_down[1])
    outs_back = jnp.stack(
        [out_cold.reshape(lines, cap, width), out_hot.reshape(lines, cap, width)], axis=1
    )
    dxs_back = jnp.stack(
        [dx_cold.reshape(lines, cap, width), dx_hot.reshape(lines, cap, width)], axis=1
    )
    outs_back = outs_back.reshape(lines, 2 * cap, width)
    dxs_back = dxs_back.reshape(lines, 2 * cap, width)
    home_out, home_dx = (
        lax.all_to_all(outs_back, "local", split_axis=0, concat_axis=0, tiled=True),
        lax.all_to_all(dxs_back, "local", split_axis=0, concat_axis=0, tiled=True),
    )
    home_out = home_out.reshape(slots * cap, width)
    home_dx = home_dx.reshape(slots * cap, width)
    gathered = lax.dot_general(placer, home_out, CONTRACT_ZERO, preferred_element_type=jnp.float32)
    gathered = gathered.reshape(tok, top, width)
    partial_out = jnp.sum(weights[:, :, None] * gathered, axis=1)
    partial_dx = lax.dot_general(
        token_placer, home_dx, CONTRACT_ZERO, preferred_element_type=jnp.float32
    )
    partial_dots = jnp.sum(cotangent.astype(jnp.float32)[:, None, :] * gathered, axis=2)
    mixed, grad_tokens = (
        lax.psum_scatter(
            partial_out.astype(jnp.bfloat16), "group", scatter_dimension=1, tiled=True
        ).astype(jnp.float32),
        lax.psum_scatter(
            partial_dx.astype(jnp.bfloat16), "group", scatter_dimension=1, tiled=True
        ).astype(jnp.float32),
    )
    gate_dots = lax.psum(partial_dots, "group")
    grad_logits = pull_back(gate_dots)[0]
    partner_bit = lax.axis_size("local").bit_length() - 2
    other = swapped((grads_hot[0], grads_hot[1], grads_hot[2]), "local", partner_bit)
    joined = [
        (mine.astype(jnp.float32) + theirs.astype(jnp.float32)).astype(jnp.bfloat16)
        for mine, theirs in zip(grads_hot, other)
    ]
    grad_gate = jnp.stack([grads_cold[0], joined[0]], axis=0)
    grad_up = jnp.stack([grads_cold[1], joined[1]], axis=0)
    grad_down = jnp.stack([grads_cold[2], joined[2]], axis=0)
    return (
        mixed.astype(jnp.bfloat16),
        grad_tokens.astype(jnp.bfloat16),
        grad_logits,
        grad_gate,
        grad_up,
        grad_down,
    )


def solution(mesh):
    return jax.shard_map(
        per_device,
        mesh=mesh,
        in_specs=(
            P("local", None),
            P("local", None),
            P("local", None),
            P("local", None),
            P(),
            P("local", None, "group"),
            P("local", None, "group"),
            P("local", "group", None),
        ),
        out_specs=(
            P("local", "group"),
            P("local", "group"),
            P("local", None),
            P("local", None, "group"),
            P("local", None, "group"),
            P("local", "group", None),
        ),
        check_vma=False,
    )
```

profile of v0, /device:TPU:0, one launch (start us, length us, event | category | flops | bytes accessed | tf_op | source)
XLA Modules:
  0.0 620.1 jit_solution(16297483419287537097)
XLA Ops:
  9.5 5.0 convolution_convert_fusion.1
  14.5 7.3 %all-to-all-start = ((bf16[16,32,7168]{2,1,0:T(8,128)(2,1)}), bf16[16,32,7168]{2,1,0:T(8,128)(2,1)}, u32[]{:S(2)}, u32[]{:S(2)}) async-start(bf16[16,32,7168]{2,1,0:T(8,128)(2,1)} %bitcast.142), calls=%async_computation | async-start | bytes 14680064 | tf_op jit(solution)/shard_map/all_to_all | solution.py:89
  22.9 5.2 convolution_convert_fusion
  28.1 102.3 %all-to-all-done = bf16[16,32,7168]{2,1,0:T(8,128)(2,1)} async-done(((bf16[16,32,7168]{2,1,0:T(8,128)(2,1)}), bf16[16,32,7168]{2,1,0:T(8,128)(2,1)}, u32[]{:S(2)}, u32[]{:S(2)}) %all-to-all-start) | async-done | bytes 7340064 | tf_op jit(solution)/shard_map/all_to_all | solution.py:89
  130.5 5.8 all-to-all-start.2
  136.3 3.8 fusion.60
  148.3 94.5 %all-to-all-done.2 = bf16[16,32,7168]{2,1,0:T(8,128)(2,1)} async-done(((bf16[16,32,7168]{2,1,0:T(8,128)(2,1)}), bf16[16,32,7168]{2,1,0:T(8,128)(2,1)}, u32[]{:S(2)}, u32[]{:S(2)}) %all-to-all-start.2) | async-done | bytes 7340064 | tf_op jit(solution)/shard_map/all_to_all | solution.py:90
  242.8 3.8 fusion.59
  258.0 3.8 pad_maximum_fusion.1
  261.8 4.9 all-to-all-start.3
  266.7 4.2 convolution_convert_fusion.4
  294.9 77.8 %all-to-all-done.3 = bf16[16,32,7168]{2,1,0:T(8,128)(2,1)} async-done(((bf16[16,32,7168]{2,1,0:T(8,128)(2,1)}), bf16[16,32,7168]{2,1,0:T(8,128)(2,1)}, u32[]{:S(2)}, u32[]{:S(2)}) %all-to-all-start.3) | async-done | bytes 7340064 | tf_op jit(solution)/shard_map/all_to_all | solution.py:112
  372.7 10.7 %all-to-all-start.1 = ((bf16[16,32,7168]{2,1,0:T(8,128)(2,1)}), bf16[16,32,7168]{2,1,0:T(8,128)(2,1)}, u32[]{:S(2)}, u32[]{:S(2)}) async-start(bf16[16,32,7168]{2,1,0:T(8,128)(2,1)} %bitcast.144), calls=%async_computation.1 | async-start | bytes 14680064 | tf_op jit(solution)/shard_map/all_to_all | solution.py:111
  383.8 58.0 %collective-permute-done.2 = bf16[128,7168]{1,0:T(8,128)(2,1)} collective-permute-done((bf16[128,7168]{1,0:T(8,128)(2,1)}, bf16[128,7168]{1,0:T(8,128)(2,1)}, u32[]{:S(2)}, u32[]{:S(2)}) %collective-permute-start.2) | collective-permute-done | bytes 1835040 | tf_op jit(solution)/shard_map/ppermute | solution.py:18
  446.5 44.4 %collective-permute-done.1 = bf16[7168,128]{1,0:T(8,128)(2,1)} collective-permute-done((bf16[7168,128]{1,0:T(8,128)(2,1)}, bf16[7168,128]{1,0:T(8,128)(2,1)}, u32[]{:S(2)}, u32[]{:S(2)}) %collective-permute-start.1) | collective-permute-done | bytes 1835040 | tf_op jit(solution)/shard_map/ppermute | solution.py:18
  490.9 3.7 fusion.10
  494.6 35.5 %collective-permute-done = bf16[7168,128]{1,0:T(8,128)(2,1)} collective-permute-done((bf16[7168,128]{1,0:T(8,128)(2,1)S(1)}, bf16[7168,128]{1,0:T(8,128)(2,1)}, u32[]{:S(2)}, u32[]{:S(2)}) %collective-permute-start) | collective-permute-done | bytes 1835040 | tf_op jit(solution)/shard_map/ppermute | solution.py:18
  533.4 4.5 convolution_convert_fusion.10
  539.8 3.7 pad_maximum_fusion.3
  543.5 4.1 all-to-all-done.1
  547.5 7.9 %multiply_reduce_fusion = (f32[32,8]{1,0:T(8,128)S(1)}, bf16[32,7168]{1,0:T(8,128)(2,1)S(1)}) fusion(f32[32,7168]{1,0:T(8,128)S(1)} %convert_element_type.121, f32[32,8]{1,0:T(8,128)S(1)} %copy.51, bf16[512,7168,1]{1,0,2:T(8,128)(2,1)} %bitcast.18, s32[256]{0:T(256)S(1)} %multiply_add_fusion.1), kind=kOutput, calls=%fused_computation.22 | convolution fusion | flops 1886289664 | bytes 8719360 | tf_op jit(solution)/shard_map/dot_general | solution.py:116
  557.4 3.7 pad_maximum_fusion.2
  561.2 14.0 %psum.7 = f32[32,8]{0,1:T(8,128)S(1)} all-reduce(f32[32,8]{0,1:T(8,128)S(1)} %copy.61), channel_id=1, replica_groups=mesh['group'=8,'local'=16] {'group'}, use_global_device_ids=true, to_apply=%region_11.12 | all-reduce | flops 256 | bytes 2048 | tf_op jit(solution)/shard_map/psum | solution.py:131
  578.8 32.8 %reduce-scatter.7.cloned.1.call-done = bf16[896,32]{1,0:T(8,128)(2,1)} async-done(((bf16[7168,32]{1,0:T(8,128)(2,1)}), bf16[896,32]{1,0:T(8,128)(2,1)}) %reduce-scatter.7.cloned.1.call-update) | async-done | bytes 57360
  (102 shorter events, 64.2 us)
Async XLA Ops:
  14.5 7.3 %copy-start.20 = (s32[32]{0:T(128)S(1)}, s32[32]{0:T(128)}, u32[]{:S(2)}) copy-start(s32[32]{0:T(128)} %param.12) | copy-start | bytes 388
  14.5 8.1 %copy-start.19 = (f32[32,24]{0,1:T(8,128)S(1)}, f32[32,24]{0,1:T(8,128)}, u32[]{:S(2)}) copy-start(f32[32,24]{0,1:T(8,128)} %param.10) | copy-start | bytes 9220
  14.5 8.3 %copy-start.18 = (bf16[32,7168]{1,0:T(8,128)(2,1)S(1)}, bf16[32,7168]{1,0:T(8,128)(2,1)}, u32[]{:S(2)}) copy-start(bf16[32,7168]{1,0:T(8,128)(2,1)} %param.9) | copy-start | bytes 1376260
  14.5 116.0 %all-to-all-start = ((bf16[16,32,7168]{2,1,0:T(8,128)(2,1)}), bf16[16,32,7168]{2,1,0:T(8,128)(2,1)}, u32[]{:S(2)}, u32[]{:S(2)}) async-start(bf16[16,32,7168]{2,1,0:T(8,128)(2,1)} %bitcast.142), calls=%async_computation | async-start | bytes 14680064 | tf_op jit(solution)/shard_map/all_to_all | solution.py:89
  130.5 112.4 %all-to-all-start.2 = ((bf16[16,32,7168]{2,1,0:T(8,128)(2,1)}), bf16[16,32,7168]{2,1,0:T(8,128)(2,1)}, u32[]{:S(2)}, u32[]{:S(2)}) async-start(bf16[16,32,7168]{2,1,0:T(8,128)(2,1)} %bitcast.143), calls=%async_computation.2 | async-start | bytes 14680064 | tf_op jit(solution)/shard_map/all_to_all | solution.py:90
  136.3 4.2 copy-start.12
  140.1 5.9 copy-start.4
  140.1 7.0 %copy-start.2 = (bf16[16,1,16,7168]{3,2,1,0:T(8,128)(2,1)}, bf16[16,1,16,7168]{3,2,1,0:T(8,128)(2,1)S(1)}, u32[]{:S(2)}) copy-start(bf16[16,1,16,7168]{3,2,1,0:T(8,128)(2,1)S(1)} %get-tuple-element.10) | copy-start | bytes 11010052
  140.1 4.8 copy-start.14
  242.8 4.2 copy-start.16
  246.6 5.9 copy-start.6
  246.6 5.9 copy-start.8
  246.6 4.8 copy-start.15
  261.8 111.0 %all-to-all-start.3 = ((bf16[16,32,7168]{2,1,0:T(8,128)(2,1)}), bf16[16,32,7168]{2,1,0:T(8,128)(2,1)}, u32[]{:S(2)}, u32[]{:S(2)}) async-start(bf16[16,32,7168]{2,1,0:T(8,128)(2,1)} %bitcast.145), calls=%async_computation.3 | async-start | bytes 14680064 | tf_op jit(solution)/shard_map/all_to_all | solution.py:112
  266.6 7.6 %copy-start.3 = (bf16[16,1,16,7168]{3,2,1,0:T(8,128)(2,1)S(1)}, bf16[16,1,16,7168]{3,2,1,0:T(8,128)(2,1)}, u32[]{:S(2)}) copy-start(bf16[16,1,16,7168]{3,2,1,0:T(8,128)(2,1)} %copy-done.2) | copy-start | bytes 11010052
  270.9 170.9 %collective-permute-start.2 = (bf16[128,7168]{1,0:T(8,128)(2,1)}, bf16[128,7168]{1,0:T(8,128)(2,1)}, u32[]{:S(2)}, u32[]{:S(2)}) collective-permute-start(bf16[128,7168]{1,0:T(8,128)(2,1)} %convolution_convert_fusion.4), channel_id=1, source_target_pairs={{0,8},{8,0},{1,9},{9,1},{2,10},{10,2},{3,11},{11,3},{4,12},{12,4},... | collective-permute-start | bytes 5505032 | tf_op jit(solution)/shard_map/ppermute | solution.py:18
  282.7 6.3 %copy-start.17 = (bf16[2,128,7168]{2,1,0:T(8,128)(2,1)S(1)}, bf16[2,128,7168]{2,1,0:T(8,128)(2,1)}, u32[]{:S(2)}) copy-start(bf16[2,128,7168]{2,1,0:T(8,128)(2,1)} %param.15) | copy-start | bytes 11010052
  285.5 205.4 %collective-permute-start.1 = (bf16[7168,128]{1,0:T(8,128)(2,1)}, bf16[7168,128]{1,0:T(8,128)(2,1)}, u32[]{:S(2)}, u32[]{:S(2)}) collective-permute-start(bf16[7168,128]{1,0:T(8,128)(2,1)} %convolution_convert_fusion.6), channel_id=1, source_target_pairs={{0,8},{8,0},{1,9},{9,1},{2,10},{10,2},{3,11},{11,3},{4,12},{12,4},... | collective-permute-start | bytes 5505032 | tf_op jit(solution)/shard_map/ppermute | solution.py:18
  285.6 244.5 %collective-permute-start = (bf16[7168,128]{1,0:T(8,128)(2,1)S(1)}, bf16[7168,128]{1,0:T(8,128)(2,1)}, u32[]{:S(2)}, u32[]{:S(2)}) collective-permute-start(bf16[7168,128]{1,0:T(8,128)(2,1)S(1)} %convolution_convert_fusion.8), channel_id=1, source_target_pairs={{0,8},{8,0},{1,9},{9,1},{2,10},{10,2},{3,11},{11,3},{4,12},{12,4},... | collective-permute-start | bytes 5505032 | tf_op jit(solution)/shard_map/ppermute | solution.py:18
  372.7 174.8 %all-to-all-start.1 = ((bf16[16,32,7168]{2,1,0:T(8,128)(2,1)}), bf16[16,32,7168]{2,1,0:T(8,128)(2,1)}, u32[]{:S(2)}, u32[]{:S(2)}) async-start(bf16[16,32,7168]{2,1,0:T(8,128)(2,1)} %bitcast.144), calls=%async_computation.1 | async-start | bytes 14680064 | tf_op jit(solution)/shard_map/all_to_all | solution.py:111
  383.5 193.7 %reduce-scatter.9.cloned.1.call-start = ((), (), s32[]{:S(2)}) async-start(), calls=%async_computation.7 | async-start | bytes 2064384
  383.8 60.5 %copy-start.11 = (bf16[1,128,7168]{2,1,0:T(8,128)(2,1)S(1)}, bf16[1,128,7168]{2,1,0:T(8,128)(2,1)}, u32[]{:S(2)}) copy-start(bf16[1,128,7168]{2,1,0:T(8,128)(2,1)} %fusion.4) | copy-start | bytes 5505028
  539.6 72.0 %reduce-scatter.7.cloned.1.call-start = ((), (), s32[]{:S(2)}) async-start(), calls=%async_computation.6 | async-start | bytes 2064384
  557.4 55.9 %copy-start.1 = (bf16[32,7168]{1,0:T(8,128)(2,1)S(1)}, bf16[32,7168]{1,0:T(8,128)(2,1)}, u32[]{:S(2)}) copy-start(bf16[32,7168]{1,0:T(8,128)(2,1)} %param.8) | copy-start | bytes 1376260
  (6 other events, 12.6 us)
Sparse Core Ops, SparseCore 0:
  539.7 37.4 reduce-scatter.8
  579.6 31.9 reduce-scatter.6
where the time goes:
time: 621 us; the launch traced here: 620 us
  waiting for transfers between devices  451 us (73%)
  matrix products  50.6 us (8%)
  starting transfers between devices  36 us (6%)
  other arithmetic  29 us (5%)
  local copies, waits for them, and re-layouts  25.2 us (4%)
  between operations  14.5 us (2%)
  blocking collectives  14 us (2%)
    ppermute x3, waiting for transfers between devices, swapped(): return lax.ppermute(block, axis, route)  138 us
    all_to_all x1, waiting for transfers between devices, per_device(): lax.all_to_all(x_buffer, 'local', split_axis=0, concat_axis=0, tiled=True)  102 us
    all_to_all x1, waiting for transfers between devices, per_device(): lax.all_to_all(g_buffer, 'local', split_axis=0, concat_axis=0, tiled=True)  94.5 us
    all_to_all x1, waiting for transfers between devices, per_device(): lax.all_to_all(dxs_back, 'local', split_axis=0, concat_axis=0, tiled=True)  77.8 us
    unnamed x4, waiting for transfers between devices  34.1 us
    unnamed x47, local copies, waits for them, and re-layouts  17 us
    psum x1, blocking collectives, per_device(): gate_dots = lax.psum(partial_dots, 'group')  14 us
  transfers between devices with their start and end apart: 9, of which 9 were waited for; matrix products, arithmetic and copies ran while one was open for 12% of the time, Pallas kernels for 0%

commit v1 on v0

--- a/solution.py
+++ b/solution.py
@@ -1,11 +1,22 @@
+import functools
 import jax
 import jax.numpy as jnp
 from jax import lax
 from jax.sharding import PartitionSpec as P
+from jax.lax import all_gather
 
 ROUTE_SCALE = 2.5
 CONTRACT_ONE = (((1,), (1,)), ((), ()))
 CONTRACT_ZERO = (((0,), (0,)), ((), ()))
+
+
+def _treat_strings(tile_in, chip_axis):
+    outer = all_gather(tile_in, chip_axis)
+    b_next = jnp.sum(outer, axis=0)
+    return b_next
+
+
+read_the_threads = functools.partial(_treat_strings, chip_axis="group")
 
 
 def swapped(block, axis, apart):
@@ -128,7 +139,7 @@
             partial_dx.astype(jnp.bfloat16), "group", scatter_dimension=1, tiled=True
         ).astype(jnp.float32),
     )
-    gate_dots = lax.psum(partial_dots, "group")
+    gate_dots = read_the_threads(partial_dots)
     grad_logits = pull_back(gate_dots)[0]
     partner_bit = lax.axis_size("local").bit_length() - 2
     other = swapped((grads_hot[0], grads_hot[1], grads_hot[2]), "local", partner_bit)

time: 621 us -> 621 us (level)
    all_gather x0 -> x1, blocking collectives: none -> 14 us  [_treat_strings(): outer = all_gather(tile_in, chip_axis)]
    psum x1 -> x0, blocking collectives: 14 us -> none  [per_device(): gate_dots = lax.psum(partial_dots, 'group')]
    unnamed x47 -> x48, local copies, waits for them, and re-layouts: 17 us -> 17 us
where the time goes in v1:
time: 621 us; the launch traced here: 620 us
  waiting for transfers between devices  451 us (73%)
  matrix products  50.6 us (8%)
  starting transfers between devices  36 us (6%)
  other arithmetic  29 us (5%)
  local copies, waits for them, and re-layouts  25.2 us (4%)
  between operations  14.5 us (2%)
  blocking collectives  14 us (2%)
    ppermute x3, waiting for transfers between devices, swapped(): return lax.ppermute(block, axis, route)  138 us
    all_to_all x1, waiting for transfers between devices, per_device(): lax.all_to_all(x_buffer, 'local', split_axis=0, concat_axis=0, tiled=True)  102 us
    all_to_all x1, waiting for transfers between devices, per_device(): lax.all_to_all(g_buffer, 'local', split_axis=0, concat_axis=0, tiled=True)  94.5 us
    all_to_all x1, waiting for transfers between devices, per_device(): lax.all_to_all(dxs_back, 'local', split_axis=0, concat_axis=0, tiled=True)  77.8 us
    unnamed x4, waiting for transfers between devices  34.1 us
    unnamed x48, local copies, waits for them, and re-layouts  17 us
    all_gather x1, blocking collectives, _treat_strings(): outer = all_gather(tile_in, chip_axis)  14 us
  transfers between devices with their start and end apart: 9, of which 9 were waited for; matrix products, arithmetic and copies ran while one was open for 12% of the time, Pallas kernels for 0%

profile of v1, /device:TPU:0, one launch (start us, length us, event | category | flops | bytes accessed | tf_op | source)
XLA Modules:
  0.0 620.1 jit_solution(2913686992960729307)
XLA Ops:
  9.5 5.0 convolution_convert_fusion.1
  14.5 7.3 %all-to-all-start = ((bf16[16,32,7168]{2,1,0:T(8,128)(2,1)}), bf16[16,32,7168]{2,1,0:T(8,128)(2,1)}, u32[]{:S(2)}, u32[]{:S(2)}) async-start(bf16[16,32,7168]{2,1,0:T(8,128)(2,1)} %bitcast.143), calls=%async_computation | async-start | bytes 14680064 | tf_op jit(solution)/shard_map/all_to_all | solution.py:100
  22.9 5.2 convolution_convert_fusion
  28.1 102.3 %all-to-all-done = bf16[16,32,7168]{2,1,0:T(8,128)(2,1)} async-done(((bf16[16,32,7168]{2,1,0:T(8,128)(2,1)}), bf16[16,32,7168]{2,1,0:T(8,128)(2,1)}, u32[]{:S(2)}, u32[]{:S(2)}) %all-to-all-start) | async-done | bytes 7340064 | tf_op jit(solution)/shard_map/all_to_all | solution.py:100
  130.5 5.8 all-to-all-start.2
  136.3 3.8 fusion.60
  148.3 94.5 %all-to-all-done.2 = bf16[16,32,7168]{2,1,0:T(8,128)(2,1)} async-done(((bf16[16,32,7168]{2,1,0:T(8,128)(2,1)}), bf16[16,32,7168]{2,1,0:T(8,128)(2,1)}, u32[]{:S(2)}, u32[]{:S(2)}) %all-to-all-start.2) | async-done | bytes 7340064 | tf_op jit(solution)/shard_map/all_to_all | solution.py:101
  242.8 3.8 fusion.59
  258.0 3.8 pad_maximum_fusion.1
  261.8 4.9 all-to-all-start.3
  266.7 4.2 convolution_convert_fusion.4
  294.9 77.8 %all-to-all-done.3 = bf16[16,32,7168]{2,1,0:T(8,128)(2,1)} async-done(((bf16[16,32,7168]{2,1,0:T(8,128)(2,1)}), bf16[16,32,7168]{2,1,0:T(8,128)(2,1)}, u32[]{:S(2)}, u32[]{:S(2)}) %all-to-all-start.3) | async-done | bytes 7340064 | tf_op jit(solution)/shard_map/all_to_all | solution.py:123
  372.7 10.7 %all-to-all-start.1 = ((bf16[16,32,7168]{2,1,0:T(8,128)(2,1)}), bf16[16,32,7168]{2,1,0:T(8,128)(2,1)}, u32[]{:S(2)}, u32[]{:S(2)}) async-start(bf16[16,32,7168]{2,1,0:T(8,128)(2,1)} %bitcast.145), calls=%async_computation.1 | async-start | bytes 14680064 | tf_op jit(solution)/shard_map/all_to_all | solution.py:122
  383.8 58.0 %collective-permute-done.2 = bf16[128,7168]{1,0:T(8,128)(2,1)} collective-permute-done((bf16[128,7168]{1,0:T(8,128)(2,1)}, bf16[128,7168]{1,0:T(8,128)(2,1)}, u32[]{:S(2)}, u32[]{:S(2)}) %collective-permute-start.2) | collective-permute-done | bytes 1835040 | tf_op jit(solution)/shard_map/ppermute | solution.py:29
  446.5 44.4 %collective-permute-done.1 = bf16[7168,128]{1,0:T(8,128)(2,1)} collective-permute-done((bf16[7168,128]{1,0:T(8,128)(2,1)}, bf16[7168,128]{1,0:T(8,128)(2,1)}, u32[]{:S(2)}, u32[]{:S(2)}) %collective-permute-start.1) | collective-permute-done | bytes 1835040 | tf_op jit(solution)/shard_map/ppermute | solution.py:29
  490.9 3.7 fusion.10
  494.6 35.5 %collective-permute-done = bf16[7168,128]{1,0:T(8,128)(2,1)} collective-permute-done((bf16[7168,128]{1,0:T(8,128)(2,1)S(1)}, bf16[7168,128]{1,0:T(8,128)(2,1)}, u32[]{:S(2)}, u32[]{:S(2)}) %collective-permute-start) | collective-permute-done | bytes 1835040 | tf_op jit(solution)/shard_map/ppermute | solution.py:29
  533.4 4.5 convolution_convert_fusion.10
  539.8 3.7 pad_maximum_fusion.3
  543.5 4.1 all-to-all-done.1
  547.5 7.9 %multiply_reduce_fusion = (f32[32,8]{1,0:T(8,128)S(1)}, bf16[32,7168]{1,0:T(8,128)(2,1)S(1)}) fusion(f32[32,7168]{1,0:T(8,128)S(1)} %convert_element_type.121, f32[32,8]{1,0:T(8,128)S(1)} %copy.53, bf16[512,7168,1]{1,0,2:T(8,128)(2,1)} %bitcast.18, s32[256]{0:T(256)S(1)} %multiply_add_fusion.1), kind=kOutput, calls=%fused_computation.22 | convolution fusion | flops 1886289664 | bytes 8719360 | tf_op jit(solution)/shard_map/dot_general | solution.py:127
  557.4 3.7 pad_maximum_fusion.2
  561.2 14.0 %all-gather.1 = f32[8,32,8]{1,2,0:T(8,128)S(1)} all-gather(f32[1,32,8]{1,2,0:T(8,128)S(1)} %copy.63), channel_id=2, replica_groups=mesh['group'=8,'local'=16] {'group'}, dimensions={0}, use_global_device_ids=true | all-gather | bytes 9216 | tf_op jit(solution)/shard_map/all_gather | solution.py:14
  578.8 32.8 %reduce-scatter.7.cloned.1.call-done = bf16[896,32]{1,0:T(8,128)(2,1)} async-done(((bf16[7168,32]{1,0:T(8,128)(2,1)}), bf16[896,32]{1,0:T(8,128)(2,1)}) %reduce-scatter.7.cloned.1.call-update) | async-done | bytes 57360
  (103 shorter events, 64.1 us)
Async XLA Ops:
  14.5 7.3 %copy-start.20 = (s32[32]{0:T(128)S(1)}, s32[32]{0:T(128)}, u32[]{:S(2)}) copy-start(s32[32]{0:T(128)} %param.12) | copy-start | bytes 388
  14.5 8.1 %copy-start.19 = (f32[32,24]{0,1:T(8,128)S(1)}, f32[32,24]{0,1:T(8,128)}, u32[]{:S(2)}) copy-start(f32[32,24]{0,1:T(8,128)} %param.10) | copy-start | bytes 9220
  14.5 8.3 %copy-start.18 = (bf16[32,7168]{1,0:T(8,128)(2,1)S(1)}, bf16[32,7168]{1,0:T(8,128)(2,1)}, u32[]{:S(2)}) copy-start(bf16[32,7168]{1,0:T(8,128)(2,1)} %param.9) | copy-start | bytes 1376260
  14.5 116.0 %all-to-all-start = ((bf16[16,32,7168]{2,1,0:T(8,128)(2,1)}), bf16[16,32,7168]{2,1,0:T(8,128)(2,1)}, u32[]{:S(2)}, u32[]{:S(2)}) async-start(bf16[16,32,7168]{2,1,0:T(8,128)(2,1)} %bitcast.143), calls=%async_computation | async-start | bytes 14680064 | tf_op jit(solution)/shard_map/all_to_all | solution.py:100
  130.5 112.4 %all-to-all-start.2 = ((bf16[16,32,7168]{2,1,0:T(8,128)(2,1)}), bf16[16,32,7168]{2,1,0:T(8,128)(2,1)}, u32[]{:S(2)}, u32[]{:S(2)}) async-start(bf16[16,32,7168]{2,1,0:T(8,128)(2,1)} %bitcast.144), calls=%async_computation.2 | async-start | bytes 14680064 | tf_op jit(solution)/shard_map/all_to_all | solution.py:101
  136.3 4.2 copy-start.12
  140.1 5.9 copy-start.4
  140.1 7.0 %copy-start.2 = (bf16[16,1,16,7168]{3,2,1,0:T(8,128)(2,1)}, bf16[16,1,16,7168]{3,2,1,0:T(8,128)(2,1)S(1)}, u32[]{:S(2)}) copy-start(bf16[16,1,16,7168]{3,2,1,0:T(8,128)(2,1)S(1)} %get-tuple-element.10) | copy-start | bytes 11010052
  140.1 4.8 copy-start.14
  242.8 4.2 copy-start.16
  246.6 5.9 copy-start.6
  246.6 5.9 copy-start.8
  246.6 4.8 copy-start.15
  261.8 111.0 %all-to-all-start.3 = ((bf16[16,32,7168]{2,1,0:T(8,128)(2,1)}), bf16[16,32,7168]{2,1,0:T(8,128)(2,1)}, u32[]{:S(2)}, u32[]{:S(2)}) async-start(bf16[16,32,7168]{2,1,0:T(8,128)(2,1)} %bitcast.146), calls=%async_computation.3 | async-start | bytes 14680064 | tf_op jit(solution)/shard_map/all_to_all | solution.py:123
  266.6 7.6 %copy-start.3 = (bf16[16,1,16,7168]{3,2,1,0:T(8,128)(2,1)S(1)}, bf16[16,1,16,7168]{3,2,1,0:T(8,128)(2,1)}, u32[]{:S(2)}) copy-start(bf16[16,1,16,7168]{3,2,1,0:T(8,128)(2,1)} %copy-done.2) | copy-start | bytes 11010052
  270.9 170.9 %collective-permute-start.2 = (bf16[128,7168]{1,0:T(8,128)(2,1)}, bf16[128,7168]{1,0:T(8,128)(2,1)}, u32[]{:S(2)}, u32[]{:S(2)}) collective-permute-start(bf16[128,7168]{1,0:T(8,128)(2,1)} %convolution_convert_fusion.4), channel_id=1, source_target_pairs={{0,8},{8,0},{1,9},{9,1},{2,10},{10,2},{3,11},{11,3},{4,12},{12,4},... | collective-permute-start | bytes 5505032 | tf_op jit(solution)/shard_map/ppermute | solution.py:29
  282.7 6.3 %copy-start.17 = (bf16[2,128,7168]{2,1,0:T(8,128)(2,1)S(1)}, bf16[2,128,7168]{2,1,0:T(8,128)(2,1)}, u32[]{:S(2)}) copy-start(bf16[2,128,7168]{2,1,0:T(8,128)(2,1)} %param.15) | copy-start | bytes 11010052
  285.5 205.4 %collective-permute-start.1 = (bf16[7168,128]{1,0:T(8,128)(2,1)}, bf16[7168,128]{1,0:T(8,128)(2,1)}, u32[]{:S(2)}, u32[]{:S(2)}) collective-permute-start(bf16[7168,128]{1,0:T(8,128)(2,1)} %convolution_convert_fusion.6), channel_id=1, source_target_pairs={{0,8},{8,0},{1,9},{9,1},{2,10},{10,2},{3,11},{11,3},{4,12},{12,4},... | collective-permute-start | bytes 5505032 | tf_op jit(solution)/shard_map/ppermute | solution.py:29
  285.6 244.5 %collective-permute-start = (bf16[7168,128]{1,0:T(8,128)(2,1)S(1)}, bf16[7168,128]{1,0:T(8,128)(2,1)}, u32[]{:S(2)}, u32[]{:S(2)}) collective-permute-start(bf16[7168,128]{1,0:T(8,128)(2,1)S(1)} %convolution_convert_fusion.8), channel_id=1, source_target_pairs={{0,8},{8,0},{1,9},{9,1},{2,10},{10,2},{3,11},{11,3},{4,12},{12,4},... | collective-permute-start | bytes 5505032 | tf_op jit(solution)/shard_map/ppermute | solution.py:29
  372.7 174.8 %all-to-all-start.1 = ((bf16[16,32,7168]{2,1,0:T(8,128)(2,1)}), bf16[16,32,7168]{2,1,0:T(8,128)(2,1)}, u32[]{:S(2)}, u32[]{:S(2)}) async-start(bf16[16,32,7168]{2,1,0:T(8,128)(2,1)} %bitcast.145), calls=%async_computation.1 | async-start | bytes 14680064 | tf_op jit(solution)/shard_map/all_to_all | solution.py:122
  383.5 193.7 %reduce-scatter.9.cloned.1.call-start = ((), (), s32[]{:S(2)}) async-start(), calls=%async_computation.7 | async-start | bytes 2064384
  383.8 60.5 %copy-start.11 = (bf16[1,128,7168]{2,1,0:T(8,128)(2,1)S(1)}, bf16[1,128,7168]{2,1,0:T(8,128)(2,1)}, u32[]{:S(2)}) copy-start(bf16[1,128,7168]{2,1,0:T(8,128)(2,1)} %fusion.4) | copy-start | bytes 5505028
  539.6 72.0 %reduce-scatter.7.cloned.1.call-start = ((), (), s32[]{:S(2)}) async-start(), calls=%async_computation.6 | async-start | bytes 2064384
  557.4 55.9 %copy-start.1 = (bf16[32,7168]{1,0:T(8,128)(2,1)S(1)}, bf16[32,7168]{1,0:T(8,128)(2,1)}, u32[]{:S(2)}) copy-start(bf16[32,7168]{1,0:T(8,128)(2,1)} %param.8) | copy-start | bytes 1376260
  (6 other events, 12.6 us)
Sparse Core Ops, SparseCore 0:
  539.7 37.3 reduce-scatter.8
  579.5 32.0 reduce-scatter.6
